TPU v7x, 32 devices: a whole 2x2x4 slice. The times are simulated.
32 devices in a mesh: pipe: 2 (over core), dp: 16 (over z, y, x).
Axes of the slice: x: 2, y: 2, z: 4, core: 2. Of those that a mesh axis runs over, the one named last changes fastest.
Arguments:
- board_input: bfloat16 [1536, 8, 8, 256], P('dp'), may hold values from -105 to 105
- conv_weight: bfloat16 [2, 4608, 256], P('pipe', 'dp'), may hold values from -0.125 to 0.125
- norm_gains: bfloat16 [2, 512], P('pipe', 'dp'), may hold values from 0.5 to 1.5
- norm_shifts: bfloat16 [2, 512], P('pipe', 'dp'), may hold values from -3 to 3
- head_params: float32 [35840], P(('pipe', 'dp')), may hold values from -0.6 to 0.6
- policy_target: int32 [1536], P('dp'), may hold values from 0 to 4671
- legal_mask: int32 [1536, 4672], P('dp'), may hold values 0 or 1
- value_target: float32 [1536], P('dp'), may hold values from -0.9 to 0.9
Outputs:
- conv_grad: float32 [2, 4608, 256], P('pipe', 'dp')
- gain_grad: float32 [2, 512], P('pipe', 'dp')
- shift_grad: float32 [2, 512], P('pipe', 'dp')
- head_grad: float32 [35840], P(('pipe', 'dp'))
- input_grad: float32 [1536, 8, 8, 256], P('dp', None, None, 'pipe')
All inputs are finite; a program needn't handle non-finite values. No bound on the sum of `legal_mask` on one device may be relied on, other than what follows from the above.
Results may differ from a plain program's by a relative error of at most 0.0074.
Values may be sent and summed in bfloat16 or wider, within the bound.
A program may use at most 192 MiB of HBM per device.

v0:
```python
import jax
import jax.numpy as jnp
from jax import lax
from jax.sharding import PartitionSpec as P

PLANES = 73
VHIDDEN = 256
MICRO = 4
MOVES = 4672


EPSILON = 1e-05
PRECISE = lax.Precision.HIGHEST


def shifted(block, axis, distance):
    devices = range(lax.axis_size(axis))
    route = [(i - distance, i) for i in devices if i - distance in devices]
    return lax.ppermute(block, axis, route)


def offset_board(board_map, delta_row, delta_col):
    padded = jnp.pad(board_map, ((0, 0), (1, 1), (1, 1), (0, 0)))
    return padded[:, 1 + delta_row : 9 + delta_row, 1 + delta_col : 9 + delta_col, :]


def convolve(board_map, tap_weights):
    row_count = board_map.shape[0] * 64
    running = jnp.zeros((row_count, tap_weights.shape[-1]), jnp.float32)
    for offset in range(9):
        moved = offset_board(board_map, offset // 3 - 1, offset % 3 - 1).reshape(row_count, -1)
        running = running + jnp.dot(moved, tap_weights[offset], preferred_element_type=jnp.float32)
    return running.reshape(board_map.shape[:3] + (tap_weights.shape[-1],))


def convolve_back(board_map, grad_field, tap_weights):
    row_count = board_map.shape[0] * 64
    grad_rows = grad_field.reshape(row_count, -1)
    back_sum = jnp.zeros(board_map.shape, jnp.float32)
    weight_parts = []
    for offset in range(9):
        delta_row = offset // 3 - 1
        delta_col = offset % 3 - 1
        moved = offset_board(board_map, delta_row, delta_col).reshape(row_count, -1)
        weight_parts.append(
            jnp.einsum("rc,rd->cd", moved, grad_rows, preferred_element_type=jnp.float32)
        )
        partial_in = jnp.einsum(
            "rd,cd->rc", grad_rows, tap_weights[offset], preferred_element_type=jnp.float32
        )
        back_sum = back_sum + offset_board(
            partial_in.reshape(board_map.shape), -delta_row, -delta_col
        )
    return (jnp.stack(weight_parts), back_sum)


def silu_slope(field_map):
    sigmoid_val = jax.nn.sigmoid(field_map)
    return sigmoid_val * (1.0 + field_map * (1.0 - sigmoid_val))


def statistics(field_map, total_rows):
    average = lax.psum(jnp.sum(field_map, axis=(0, 1, 2)), "dp") / total_rows
    spread = lax.psum(jnp.sum(jnp.square(field_map - average), axis=(0, 1, 2)), "dp") / total_rows
    return (average, lax.rsqrt(spread + EPSILON))


def norm_backward(grad_field, normed, gain_vec, inv_spread, total_rows):
    local_shift = jnp.sum(grad_field, axis=(0, 1, 2))
    local_gain = jnp.sum(grad_field * normed, axis=(0, 1, 2))
    all_shift, all_gain = lax.psum((local_shift, local_gain), "dp")
    result = (
        gain_vec
        * inv_spread
        * (grad_field - all_shift / total_rows - normed * (all_gain / total_rows))
    )
    return (result.astype(jnp.bfloat16), local_gain, local_shift)


def block_forward(block_in, tap_weights, gain_rows, shift_rows, total_rows):
    first_conv = convolve(block_in, tap_weights[0])
    first_avg, first_inv = statistics(first_conv, total_rows)
    inner_act = jax.nn.silu(
        (first_conv - first_avg) * first_inv * gain_rows[0] + shift_rows[0]
    ).astype(jnp.bfloat16)
    second = convolve(inner_act, tap_weights[1])
    second_avg, second_inv = statistics(second, total_rows)
    block_out = jax.nn.silu(
        block_in.astype(jnp.float32)
        + (second - second_avg) * second_inv * gain_rows[1]
        + shift_rows[1]
    )
    return (
        block_out,
        (block_in, first_conv, first_avg, first_inv, inner_act, second, second_avg, second_inv),
    )


def block_backward(grad_field, kept_state, tap_weights, gain_rows, shift_rows, total_rows):
    block_in, first_conv, first_avg, first_inv, inner_act, second, second_avg, second_inv = (
        kept_state
    )
    second_norm = (second - second_avg) * second_inv
    outer_pre = block_in.astype(jnp.float32) + second_norm * gain_rows[1] + shift_rows[1]
    grad_outer = grad_field * silu_slope(outer_pre)
    grad_second, gain_second, shift_second = norm_backward(
        grad_outer, second_norm, gain_rows[1], second_inv, total_rows
    )
    weight_second, grad_inner = convolve_back(inner_act, grad_second, tap_weights[1])
    first_norm = (first_conv - first_avg) * first_inv
    grad_first_pre = grad_inner * silu_slope(first_norm * gain_rows[0] + shift_rows[0])
    grad_first, gain_first, shift_first = norm_backward(
        grad_first_pre, first_norm, gain_rows[0], first_inv, total_rows
    )
    weight_first, grad_entry = convolve_back(block_in, grad_first, tap_weights[0])
    conv_grad = jnp.stack([weight_first, weight_second]).reshape(-1, grad_field.shape[-1])
    gain_grad = jnp.concatenate([gain_first, gain_second])
    shift_grad = jnp.concatenate([shift_first, shift_second])
    return (grad_entry + grad_outer, conv_grad, gain_grad, shift_grad)


def head_loss(board_map, head_all, policy_target, legal_mask, value_target):
    per_batch = board_map.shape[0]
    channels = board_map.shape[-1]
    conv_end = (PLANES + 1) * channels
    head_conv = head_all[:conv_end].reshape(channels, PLANES + 1)
    hidden_weight = head_all[conv_end : conv_end + 64 * VHIDDEN].reshape(64, VHIDDEN)
    hidden_bias = head_all[conv_end + 64 * VHIDDEN : conv_end + 65 * VHIDDEN]
    output_weight = head_all[conv_end + 65 * VHIDDEN :]
    planes = jnp.dot(board_map.reshape(per_batch * 64, channels), head_conv, precision=PRECISE)
    logits = planes[:, :PLANES].reshape(per_batch, MOVES)
    target_hit = jnp.arange(MOVES, dtype=jnp.int32)[None, :] == policy_target[:, None]
    is_legal = jnp.logical_or(legal_mask > 0, target_hit)
    masked = jnp.where(is_legal, logits, -1e30)
    highest = jnp.max(masked, axis=1, keepdims=True)
    log_total = highest[:, 0] + jnp.log(jnp.sum(jnp.exp(masked - highest), axis=1))
    chosen = jnp.sum(jnp.where(target_hit, logits, 0.0), axis=1)
    squares = jax.nn.silu(planes[:, PLANES].reshape(per_batch, 64))
    hidden = jax.nn.silu(jnp.dot(squares, hidden_weight, precision=PRECISE) + hidden_bias)
    value_out = jnp.tanh(jnp.dot(hidden, output_weight, precision=PRECISE))
    return jnp.sum(log_total - chosen + jnp.square(value_out - value_target))


def local(
    board_input,
    conv_weight,
    norm_gains,
    norm_shifts,
    head_params,
    policy_target,
    legal_mask,
    value_target,
):
    section_index = lax.axis_index("pipe")
    is_last = section_index == 1
    is_first = section_index == 0
    channels = board_input.shape[-1]
    per_batch = board_input.shape[0] // MICRO
    total_rows = lax.axis_size("dp") * per_batch * 64
    loss_scale = jnp.asarray(1.0 / (MICRO * per_batch), jnp.float32)
    conv_all, gain_all, shift_all = (
        lax.all_gather(conv_weight, "dp", axis=1, tiled=True),
        lax.all_gather(norm_gains, "dp", axis=1, tiled=True),
        lax.all_gather(norm_shifts, "dp", axis=1, tiled=True),
    )
    tap_weights = conv_all[0].reshape(2, 9, channels, channels)
    gain_rows = gain_all[0].astype(jnp.float32).reshape(2, channels)
    shift_rows = shift_all[0].astype(jnp.float32).reshape(2, channels)
    head_all = lax.all_gather(head_params, ("pipe", "dp"), axis=0, tiled=True)
    boards = board_input.reshape(MICRO, per_batch, 8, 8, channels)
    targets = policy_target.reshape(MICRO, per_batch)
    masks = legal_mask.reshape(MICRO, per_batch, -1)
    values = value_target.reshape(MICRO, per_batch)
    arrived = jnp.zeros((per_batch, 8, 8, channels), jnp.bfloat16)
    head_sum = jnp.zeros(head_all.shape, jnp.float32)
    kept_list = []
    for stepping in range(MICRO + 1):
        block_in = jnp.where(is_first, boards[min(stepping, MICRO - 1)], arrived)
        block_out, kept_state = block_forward(
            block_in, tap_weights, gain_rows, shift_rows, total_rows
        )
        head_index = max(stepping - 1, 0)

        def batch_loss(board_map, head_vec):
            return head_loss(
                board_map, head_vec, targets[head_index], masks[head_index], values[head_index]
            )

        loss_value, pull_back = jax.vjp(batch_loss, block_out, head_all)
        grad_board, grad_heads = pull_back(loss_scale)
        head_use = is_last.astype(jnp.float32) * (1.0 if stepping >= 1 else 0.0)
        head_sum = head_sum + head_use * grad_heads
        kept_list.append((kept_state, grad_board))
        if stepping < MICRO:
            arrived = shifted(block_out.astype(jnp.bfloat16), "pipe", 1)
    returned = jnp.zeros((per_batch, 8, 8, channels), jnp.bfloat16)
    conv_share = jnp.zeros((conv_weight.shape[1], channels), jnp.float32)
    gain_share = jnp.zeros((norm_gains.shape[1],), jnp.float32)
    shift_share = jnp.zeros((norm_shifts.shape[1],), jnp.float32)
    input_list = []
    for stepping in range(MICRO + 1):
        kept_state, grad_board = kept_list[MICRO - stepping]
        grad_field = jnp.where(is_last, grad_board, returned.astype(jnp.float32))
        grad_entry, conv_grad, gain_grad, shift_grad = block_backward(
            grad_field, kept_state, tap_weights, gain_rows, shift_rows, total_rows
        )
        useful = jnp.where(
            is_last, 1.0 if stepping < MICRO else 0.0, 1.0 if stepping >= 1 else 0.0
        ).astype(jnp.float32)
        conv_part, gain_part, shift_part = (
            lax.psum_scatter(useful * conv_grad, "dp", scatter_dimension=0, tiled=True),
            lax.psum_scatter(useful * gain_grad, "dp", scatter_dimension=0, tiled=True),
            lax.psum_scatter(useful * shift_grad, "dp", scatter_dimension=0, tiled=True),
        )
        conv_share = conv_share + conv_part
        gain_share = gain_share + gain_part
        shift_share = shift_share + shift_part
        if stepping >= 1:
            input_list.append(grad_entry)
        if stepping < MICRO:
            returned = shifted(grad_entry.astype(jnp.bfloat16), "pipe", -1)
    head_share = lax.psum_scatter(head_sum, ("pipe", "dp"), scatter_dimension=0, tiled=True)
    grad_input = jnp.concatenate(input_list[::-1], axis=0)
    half_width = channels // 2
    upper_half = shifted(grad_input[..., half_width:].astype(jnp.bfloat16), "pipe", 1).astype(
        jnp.float32
    )
    input_share = jnp.where(is_first, grad_input[..., :half_width], upper_half)
    return (conv_share[None], gain_share[None], shift_share[None], head_share, input_share)


def solution(mesh):
    placed = (
        P("dp", None, None, None),
        P("pipe", "dp", None),
        P("pipe", "dp"),
        P("pipe", "dp"),
        P(("pipe", "dp")),
        P("dp"),
        P("dp", None),
        P("dp"),
    )
    return jax.shard_map(
        local,
        mesh=mesh,
        in_specs=placed,
        out_specs=(
            P("pipe", "dp", None),
            P("pipe", "dp"),
            P("pipe", "dp"),
            P(("pipe", "dp")),
            P("dp", None, None, "pipe"),
        ),
        check_vma=False,
    )
```

profile of v0, /device:TPU:0, one launch (start us, length us, event | category | flops | bytes accessed | tf_op | source)
XLA Modules:
  0.0 1917.8 jit_solution(12557447253713160261)
XLA Ops:
  14.0 43.7 %all-reduce.136 = (bf16[512]{0:T(512)(128)(2,1)S(1)}, bf16[512]{0:T(512)(128)(2,1)S(1)}) all-reduce(bf16[512]{0:T(512)(128)(2,1)S(1)} %dynamic-update-slice.1, bf16[512]{0:T(512)(128)(2,1)S(1)} %dynamic-update-slice), channel_id=1, replica_groups=mesh['pipe'=2,'dp'=16] {'dp'}, use_global_device_ids=true, to_apply=%add.121 | all-reduce | flops 1024 | bytes 4096
  75.9 69.2 %all-reduce.140.cloned.1.call-done = f32[35840]{0:T(1024)} async-done(((f32[35840]{0:T(1024)}), f32[35840]{0:T(1024)}) %all-reduce.140.cloned.1.call-update) | async-done | bytes 143376
  159.0 42.8 %psum.280 = f32[256]{0:T(256)S(1)} all-reduce(f32[256]{0:T(256)S(1)} %get-tuple-element.215), channel_id=1, replica_groups=mesh['pipe'=2,'dp'=16] {'dp'}, use_global_device_ids=true, to_apply=%region_1.2 | all-reduce | flops 256 | bytes 2048 | tf_op jit(solution)/shard_map/psum | solution.py:63
  203.5 36.8 %psum.281 = f32[256]{0:T(256)S(1)} all-reduce(f32[256]{0:T(256)S(1)} %multiply_reduce_fusion.19), channel_id=1, replica_groups=mesh['pipe'=2,'dp'=16] {'dp'}, use_global_device_ids=true, to_apply=%region_3.4 | all-reduce | flops 256 | bytes 2048 | tf_op jit(solution)/shard_map/psum | solution.py:64
  250.0 38.5 %psum.282 = f32[256]{0:T(256)S(1)} all-reduce(f32[256]{0:T(256)S(1)} %get-tuple-element.217), channel_id=1, replica_groups=mesh['pipe'=2,'dp'=16] {'dp'}, use_global_device_ids=true, to_apply=%region_5.6 | all-reduce | flops 256 | bytes 2048 | tf_op jit(solution)/shard_map/psum | solution.py:63
  347.1 38.6 %psum.284 = f32[256]{0:T(256)S(1)} all-reduce(f32[256]{0:T(256)S(1)} %get-tuple-element.219), channel_id=1, replica_groups=mesh['pipe'=2,'dp'=16] {'dp'}, use_global_device_ids=true, to_apply=%region_9.10 | all-reduce | flops 256 | bytes 2048 | tf_op jit(solution)/shard_map/psum | solution.py:63
  387.3 37.0 %psum.285 = f32[256]{0:T(256)S(1)} all-reduce(f32[256]{0:T(256)S(1)} %multiply_reduce_fusion.17), channel_id=1, replica_groups=mesh['pipe'=2,'dp'=16] {'dp'}, use_global_device_ids=true, to_apply=%region_11.12 | all-reduce | flops 256 | bytes 2048 | tf_op jit(solution)/shard_map/psum | solution.py:64
  434.0 38.5 %psum.286 = f32[256]{0:T(256)S(1)} all-reduce(f32[256]{0:T(256)S(1)} %get-tuple-element.221), channel_id=1, replica_groups=mesh['pipe'=2,'dp'=16] {'dp'}, use_global_device_ids=true, to_apply=%region_13.14 | all-reduce | flops 256 | bytes 2048 | tf_op jit(solution)/shard_map/psum | solution.py:63
  474.2 36.6 %psum.287 = f32[256]{0:T(256)S(1)} all-reduce(f32[256]{0:T(256)S(1)} %multiply_reduce_fusion.16), channel_id=1, replica_groups=mesh['pipe'=2,'dp'=16] {'dp'}, use_global_device_ids=true, to_apply=%region_15.16 | all-reduce | flops 256 | bytes 2048 | tf_op jit(solution)/shard_map/psum | solution.py:64
  530.6 38.5 %psum.288 = f32[256]{0:T(256)S(1)} all-reduce(f32[256]{0:T(256)S(1)} %get-tuple-element.223), channel_id=1, replica_groups=mesh['pipe'=2,'dp'=16] {'dp'}, use_global_device_ids=true, to_apply=%region_17.18 | all-reduce | flops 256 | bytes 2048 | tf_op jit(solution)/shard_map/psum | solution.py:63
  570.8 36.7 %psum.289 = f32[256]{0:T(256)S(1)} all-reduce(f32[256]{0:T(256)S(1)} %multiply_reduce_fusion.15), channel_id=1, replica_groups=mesh['pipe'=2,'dp'=16] {'dp'}, use_global_device_ids=true, to_apply=%region_19.20 | all-reduce | flops 256 | bytes 2048 | tf_op jit(solution)/shard_map/psum | solution.py:64
  617.3 38.5 %psum.290 = f32[256]{0:T(256)S(1)} all-reduce(f32[256]{0:T(256)S(1)} %get-tuple-element.225), channel_id=1, replica_groups=mesh['pipe'=2,'dp'=16] {'dp'}, use_global_device_ids=true, to_apply=%region_21.22 | all-reduce | flops 256 | bytes 2048 | tf_op jit(solution)/shard_map/psum | solution.py:63
  657.5 36.6 %psum.291 = f32[256]{0:T(256)S(1)} all-reduce(f32[256]{0:T(256)S(1)} %multiply_reduce_fusion.14), channel_id=1, replica_groups=mesh['pipe'=2,'dp'=16] {'dp'}, use_global_device_ids=true, to_apply=%region_23.24 | all-reduce | flops 256 | bytes 2048 | tf_op jit(solution)/shard_map/psum | solution.py:64
  714.7 38.5 %psum.292 = f32[256]{0:T(256)S(1)} all-reduce(f32[256]{0:T(256)S(1)} %get-tuple-element.227), channel_id=1, replica_groups=mesh['pipe'=2,'dp'=16] {'dp'}, use_global_device_ids=true, to_apply=%region_25.26 | all-reduce | flops 256 | bytes 2048 | tf_op jit(solution)/shard_map/psum | solution.py:63
  754.8 37.0 %psum.293 = f32[256]{0:T(256)S(1)} all-reduce(f32[256]{0:T(256)S(1)} %multiply_reduce_fusion.13), channel_id=1, replica_groups=mesh['pipe'=2,'dp'=16] {'dp'}, use_global_device_ids=true, to_apply=%region_27.28 | all-reduce | flops 256 | bytes 2048 | tf_op jit(solution)/shard_map/psum | solution.py:64
  801.6 38.5 %psum.294 = f32[256]{0:T(256)S(1)} all-reduce(f32[256]{0:T(256)S(1)} %get-tuple-element.229), channel_id=1, replica_groups=mesh['pipe'=2,'dp'=16] {'dp'}, use_global_device_ids=true, to_apply=%region_29.30 | all-reduce | flops 256 | bytes 2048 | tf_op jit(solution)/shard_map/psum | solution.py:63
  841.8 36.6 %psum.295 = f32[256]{0:T(256)S(1)} all-reduce(f32[256]{0:T(256)S(1)} %multiply_reduce_fusion.12), channel_id=1, replica_groups=mesh['pipe'=2,'dp'=16] {'dp'}, use_global_device_ids=true, to_apply=%region_31.32 | all-reduce | flops 256 | bytes 2048 | tf_op jit(solution)/shard_map/psum | solution.py:64
  899.9 38.5 %psum.296 = f32[256]{0:T(256)S(1)} all-reduce(f32[256]{0:T(256)S(1)} %get-tuple-element.231), channel_id=1, replica_groups=mesh['pipe'=2,'dp'=16] {'dp'}, use_global_device_ids=true, to_apply=%region_33.34 | all-reduce | flops 256 | bytes 2048 | tf_op jit(solution)/shard_map/psum | solution.py:63
  940.1 36.6 %psum.297 = f32[256]{0:T(256)S(1)} all-reduce(f32[256]{0:T(256)S(1)} %multiply_reduce_fusion.11), channel_id=1, replica_groups=mesh['pipe'=2,'dp'=16] {'dp'}, use_global_device_ids=true, to_apply=%region_35.36 | all-reduce | flops 256 | bytes 2048 | tf_op jit(solution)/shard_map/psum | solution.py:64
  986.3 38.6 %psum.298 = f32[256]{0:T(256)S(1)} all-reduce(f32[256]{0:T(256)S(1)} %get-tuple-element.233), channel_id=1, replica_groups=mesh['pipe'=2,'dp'=16] {'dp'}, use_global_device_ids=true, to_apply=%region_37.38 | all-reduce | flops 256 | bytes 2048 | tf_op jit(solution)/shard_map/psum | solution.py:63
  1026.6 36.7 %psum.299 = f32[256]{0:T(256)S(1)} all-reduce(f32[256]{0:T(256)S(1)} %multiply_reduce_fusion.10), channel_id=1, replica_groups=mesh['pipe'=2,'dp'=16] {'dp'}, use_global_device_ids=true, to_apply=%region_39.40 | all-reduce | flops 256 | bytes 2048 | tf_op jit(solution)/shard_map/psum | solution.py:64
  1201.9 39.0 %all-reduce.135 = (f32[256]{0:T(256)S(1)}, f32[256]{0:T(256)S(1)}) all-reduce(f32[256]{0:T(256)S(1)} %get-tuple-element.24, f32[256]{0:T(256)S(1)} %get-tuple-element.23), channel_id=1, replica_groups=mesh['pipe'=2,'dp'=16] {'dp'}, use_global_device_ids=true, to_apply=%region_51.52 | all-reduce | flops 512 | bytes 4096 | tf_op jit(solution)/shard_map/psum | solution.py:71
  1251.8 36.6 %all-reduce.134 = (f32[256]{0:T(256)S(1)}, f32[256]{0:T(256)S(1)}) all-reduce(f32[256]{0:T(256)S(1)} %get-tuple-element.22, f32[256]{0:T(256)S(1)} %get-tuple-element.21), channel_id=1, replica_groups=mesh['pipe'=2,'dp'=16] {'dp'}, use_global_device_ids=true, to_apply=%region_55.56 | all-reduce | flops 512 | bytes 4096 | tf_op jit(solution)/shard_map/psum | solution.py:71
  1327.6 38.7 %all-reduce.133 = (f32[256]{0:T(256)S(1)}, f32[256]{0:T(256)S(1)}) all-reduce(f32[256]{0:T(256)S(1)} %get-tuple-element.20, f32[256]{0:T(256)S(1)} %get-tuple-element.19), channel_id=1, replica_groups=mesh['pipe'=2,'dp'=16] {'dp'}, use_global_device_ids=true, to_apply=%region_68.69 | all-reduce | flops 512 | bytes 4096 | tf_op jit(solution)/shard_map/psum | solution.py:71
  1377.2 36.6 %all-reduce.132 = (f32[256]{0:T(256)S(1)}, f32[256]{0:T(256)S(1)}) all-reduce(f32[256]{0:T(256)S(1)} %get-tuple-element.18, f32[256]{0:T(256)S(1)} %get-tuple-element.17), channel_id=1, replica_groups=mesh['pipe'=2,'dp'=16] {'dp'}, use_global_device_ids=true, to_apply=%region_72.73 | all-reduce | flops 512 | bytes 4096 | tf_op jit(solution)/shard_map/psum | solution.py:71
  1439.9 39.0 %all-reduce.131 = (f32[256]{0:T(256)S(1)}, f32[256]{0:T(256)S(1)}) all-reduce(f32[256]{0:T(256)S(1)} %get-tuple-element.16, f32[256]{0:T(256)S(1)} %get-tuple-element.15), channel_id=1, replica_groups=mesh['pipe'=2,'dp'=16] {'dp'}, use_global_device_ids=true, to_apply=%region_85.86 | all-reduce | flops 512 | bytes 4096 | tf_op jit(solution)/shard_map/psum | solution.py:71
  1489.8 36.6 %all-reduce.130 = (f32[256]{0:T(256)S(1)}, f32[256]{0:T(256)S(1)}) all-reduce(f32[256]{0:T(256)S(1)} %get-tuple-element.14, f32[256]{0:T(256)S(1)} %get-tuple-element.13), channel_id=1, replica_groups=mesh['pipe'=2,'dp'=16] {'dp'}, use_global_device_ids=true, to_apply=%region_89.90 | all-reduce | flops 512 | bytes 4096 | tf_op jit(solution)/shard_map/psum | solution.py:71
  1552.5 38.8 %all-reduce.129 = (f32[256]{0:T(256)S(1)}, f32[256]{0:T(256)S(1)}) all-reduce(f32[256]{0:T(256)S(1)} %get-tuple-element.12, f32[256]{0:T(256)S(1)} %get-tuple-element.11), channel_id=1, replica_groups=mesh['pipe'=2,'dp'=16] {'dp'}, use_global_device_ids=true, to_apply=%region_102.103 | all-reduce | flops 512 | bytes 4096 | tf_op jit(solution)/shard_map/psum | solution.py:71
  1602.1 36.6 %all-reduce.128 = (f32[256]{0:T(256)S(1)}, f32[256]{0:T(256)S(1)}) all-reduce(f32[256]{0:T(256)S(1)} %get-tuple-element.10, f32[256]{0:T(256)S(1)} %get-tuple-element.9), channel_id=1, replica_groups=mesh['pipe'=2,'dp'=16] {'dp'}, use_global_device_ids=true, to_apply=%region_106.107 | all-reduce | flops 512 | bytes 4096 | tf_op jit(solution)/shard_map/psum | solution.py:71
  1665.7 38.7 %all-reduce.127 = (f32[256]{0:T(256)S(1)}, f32[256]{0:T(256)S(1)}) all-reduce(f32[256]{0:T(256)S(1)} %get-tuple-element.8, f32[256]{0:T(256)S(1)} %get-tuple-element.7), channel_id=1, replica_groups=mesh['pipe'=2,'dp'=16] {'dp'}, use_global_device_ids=true, to_apply=%region_119.120 | all-reduce | flops 512 | bytes 4096 | tf_op jit(solution)/shard_map/psum | solution.py:71
  1715.5 37.1 %all-reduce.126 = (f32[256]{0:T(256)S(1)}, f32[256]{0:T(256)S(1)}, f32[512]{0:T(512)S(1)}, f32[512]{0:T(512)S(1)}) all-reduce(f32[256]{0:T(256)S(1)} %get-tuple-element.6, f32[256]{0:T(256)S(1)} %get-tuple-element.5, f32[512]{0:T(512)S(1)} %fusion.624, f32[512]{0:T(512)S(1)} %fusion.628), channel_id=1, replica_groups=mesh['pipe'=2,'dp'=16] {'dp'}, use_global_device_ids=true, to_apply=%region_123.124 | all-reduce | flops 1536 | bytes 12288 | tf_op jit(solution)/shard_map/psum | solution.py:71
  1795.8 114.3 %reduce-scatter.2.cloned.1.call-done = f32[288,256]{1,0:T(8,128)} async-done(((f32[4608,256]{1,0:T(8,128)}), f32[288,256]{1,0:T(8,128)}) %reduce-scatter.2.cloned.1.call-update) | async-done | bytes 294928 | tf_op jit(solution)/shard_map/reduce_scatter | solution.py:211
  (1022 shorter events, 571.9 us)
Async XLA Ops:
  8.0 137.2 %all-reduce.140.cloned.1.call-start = ((), (), s32[]{:S(2)}) async-start(), calls=%async_computation.3 | async-start | bytes 286720
  9.7 138.2 %all-gather.2.cloned.1.call-start = ((), (), s32[]{:S(2)}) async-start(), calls=%async_computation.1 | async-start | bytes 2506752 | tf_op jit(solution)/shard_map/all_gather | solution.py:162
  10.2 1778.2 %all-reduce.142.cloned.1.call-start = ((), (), s32[]{:S(2)}) async-start(), calls=%async_computation.4 | async-start | bytes 286720
  71.8 910.1 %copy-start.115 = (f32[1,256]{1,0:T(1,128)}, f32[1,256]{1,0:T(1,128)S(1)}, u32[]{:S(2)}) copy-start(f32[1,256]{1,0:T(1,128)S(1)} %get-tuple-element.187) | copy-start | bytes 3076
  71.8 992.0 %copy-start.113 = (f32[1,256]{1,0:T(1,128)}, f32[1,256]{1,0:T(1,128)S(1)}, u32[]{:S(2)}) copy-start(f32[1,256]{1,0:T(1,128)S(1)} %get-tuple-element.188) | copy-start | bytes 3076
  71.8 910.1 %copy-start.109 = (f32[1,256]{1,0:T(1,128)}, f32[1,256]{1,0:T(1,128)S(1)}, u32[]{:S(2)}) copy-start(f32[1,256]{1,0:T(1,128)S(1)} %get-tuple-element.185) | copy-start | bytes 3076
  73.0 254.3 %copy-start.39 = (bf16[24,8,8,256]{3,2,1,0:T(8,128)(2,1)}, bf16[24,8,8,256]{3,2,1,0:T(8,128)(2,1)S(1)}, u32[]{:S(2)}) copy-start(bf16[24,8,8,256]{3,2,1,0:T(8,128)(2,1)S(1)} %slice_select_fusion.1) | copy-start | bytes 2359300
  147.9 556.1 %copy-start.167 = (f32[256]{0:T(256)}, f32[256]{0:T(256)S(1)}, u32[]{:S(2)}) copy-start(f32[256]{0:T(256)S(1)} %get-tuple-element.183) | copy-start | bytes 3076
  201.8 43.8 %copy-start.121 = (f32[256]{0:T(256)}, f32[256]{0:T(256)S(1)}, u32[]{:S(2)}) copy-start(f32[256]{0:T(256)S(1)} %broadcast_multiply_fusion.29) | copy-start | bytes 3076
  331.9 7.8 collective-permute-start
  340.9 170.5 %copy-start.30 = (bf16[24,8,8,256]{3,2,1,0:T(8,128)(2,1)}, bf16[24,8,8,256]{3,2,1,0:T(8,128)(2,1)S(1)}, u32[]{:S(2)}) copy-start(bf16[24,8,8,256]{3,2,1,0:T(8,128)(2,1)S(1)} %slice_select_fusion.2) | copy-start | bytes 2359300
  385.6 43.9 %copy-start.123 = (f32[256]{0:T(256)}, f32[256]{0:T(256)S(1)}, u32[]{:S(2)}) copy-start(f32[256]{0:T(256)S(1)} %broadcast_multiply_fusion.27) | copy-start | bytes 3076
  518.2 4.9 collective-permute-start.1
  524.4 170.3 %copy-start.33 = (bf16[24,8,8,256]{3,2,1,0:T(8,128)(2,1)}, bf16[24,8,8,256]{3,2,1,0:T(8,128)(2,1)S(1)}, u32[]{:S(2)}) copy-start(bf16[24,8,8,256]{3,2,1,0:T(8,128)(2,1)S(1)} %slice_select_fusion.3) | copy-start | bytes 2359300
  569.2 43.7 %copy-start.125 = (f32[256]{0:T(256)}, f32[256]{0:T(256)S(1)}, u32[]{:S(2)}) copy-start(f32[256]{0:T(256)S(1)} %broadcast_multiply_fusion.25) | copy-start | bytes 3076
  701.6 5.6 collective-permute-start.2
  708.4 170.5 %copy-start.36 = (bf16[24,8,8,256]{3,2,1,0:T(8,128)(2,1)}, bf16[24,8,8,256]{3,2,1,0:T(8,128)(2,1)S(1)}, u32[]{:S(2)}) copy-start(bf16[24,8,8,256]{3,2,1,0:T(8,128)(2,1)S(1)} %broadcast_select_fusion.1) | copy-start | bytes 2359300
  753.2 44.0 %copy-start.127 = (f32[256]{0:T(256)}, f32[256]{0:T(256)S(1)}, u32[]{:S(2)}) copy-start(f32[256]{0:T(256)S(1)} %broadcast_multiply_fusion.23) | copy-start | bytes 3076
  885.9 6.6 collective-permute-start.3
  893.6 303.3 %copy-start.28 = (bf16[24,8,8,256]{3,2,1,0:T(8,128)(2,1)}, bf16[24,8,8,256]{3,2,1,0:T(8,128)(2,1)S(1)}, u32[]{:S(2)}) copy-start(bf16[24,8,8,256]{3,2,1,0:T(8,128)(2,1)S(1)} %broadcast_select_fusion) | copy-start | bytes 2359300
  938.5 43.5 %copy-start.129 = (f32[256]{0:T(256)}, f32[256]{0:T(256)S(1)}, u32[]{:S(2)}) copy-start(f32[256]{0:T(256)S(1)} %broadcast_multiply_fusion.21) | copy-start | bytes 3076
  1196.9 713.2 %reduce-scatter.2.cloned.1.call-start = ((), (), s32[]{:S(2)}) async-start(), calls=%async_computation.2 | async-start | bytes 5013504 | tf_op jit(solution)/shard_map/reduce_scatter | solution.py:211
  1197.0 44.0 %copy-start.132 = (f32[256]{0:T(256)S(1)}, f32[256]{0:T(256)}, u32[]{:S(2)}) copy-start(f32[256]{0:T(256)} %copy-done.131) | copy-start | bytes 3076
  1197.0 44.0 %copy-start.152 = (f32[256]{0:T(256)S(1)}, f32[256]{0:T(256)}, u32[]{:S(2)}) copy-start(f32[256]{0:T(256)} %copy-done.151) | copy-start | bytes 3076
  1197.0 44.0 %copy-start.171 = (f32[256]{0:T(256)S(1)}, f32[256]{0:T(256)}, u32[]{:S(2)}) copy-start(f32[256]{0:T(256)} %get-tuple-element.207) | copy-start | bytes 3076
  1297.7 25.3 %collective-permute-start.4 = (bf16[24,8,8,256]{3,2,1,0:T(8,128)(2,1)}, bf16[24,8,8,256]{3,2,1,0:T(8,128)(2,1)}, u32[]{:S(2)}, u32[]{:S(2)}) collective-permute-start(bf16[24,8,8,256]{3,2,1,0:T(8,128)(2,1)} %fusion.50), channel_id=1, source_target_pairs={{16,0},{17,1},{18,2},{19,3},{20,4},{21,5},{22,6},{23,7},{24,8},{25... | collective-permute-start | bytes 2359304 | tf_op jit(solution)/shard_map/ppermute | solution.py:19
  1323.1 43.3 %copy-start.166 = (f32[256]{0:T(256)S(1)}, f32[256]{0:T(256)}, u32[]{:S(2)}) copy-start(f32[256]{0:T(256)} %get-tuple-element.203) | copy-start | bytes 3076
  1423.2 11.1 collective-permute-start.5
  1535.8 11.1 collective-permute-start.6
  1648.0 11.4 collective-permute-start.7
  1661.0 43.4 %copy-start.160 = (f32[256]{0:T(256)S(1)}, f32[256]{0:T(256)}, u32[]{:S(2)}) copy-start(f32[256]{0:T(256)} %get-tuple-element.191) | copy-start | bytes 3076
  1785.3 5.7 collective-permute-start.8
  (192 other events, 1500.8 us)
Sparse Core Ops, SparseCore 0:
  15.0 130.1 all-reduce.139
  1197.0 118.3 all-reduce.141
Sparse Core Ops, SparseCore 1:
  12.9 65.5 all-gather.1
  1774.7 135.4 reduce-scatter.1
where the time goes:
time: 1930 us; the launch traced here: 1920 us
  blocking collectives  1180 us (61%)
  matrix products  216 us (11%)
  waiting for transfers between devices  184 us (10%)
  local copies, waits for them, and re-layouts  157 us (8%)
  other arithmetic  145 us (8%)
  between operations  20.9 us (1%)
    psum x10, blocking collectives, statistics(): average = lax.psum(jnp.sum(field_map, axis=(0, 1, 2)), 'dp') / total_rows  390 us
    psum x10, blocking collectives, norm_backward(): all_shift, all_gain = lax.psum((local_shift, local_gain), 'dp')  378 us
    psum x10, blocking collectives, statistics(): lax.psum(jnp.sum(jnp.square(field_map - average), axis=(0, 1, 2)), 'dp')  367 us
    reduce_scatter x1, waiting for transfers between devices, local(): lax.psum_scatter(useful * conv_grad, 'dp', scatter_dimension=0, tiled=True)  114 us
    unnamed x6, waiting for transfers between devices  69.8 us
    unnamed x435, local copies, waits for them, and re-layouts  66.1 us
    dot_general x90, matrix products, convolve_back(): jnp.einsum('rd,cd->rc', grad_rows, tap_weights[offset], preferred_element...  58 us
    dot_general x90, matrix products, convolve(): jnp.dot(moved, tap_weights[offset], preferred_element_type=jnp.float32)  51.1 us
  transfers between devices with their start and end apart: 13, of which 2 were waited for; matrix products, arithmetic and copies ran while one was open for 11% of the time, Pallas kernels for 0%

commit v1 on v0

v1 whole, which is shorter than its diff:
```python
import functools

import jax
import jax.numpy as jnp
from jax import lax
from jax.experimental import pallas as pl
from jax.experimental.pallas import tpu as pltpu
from jax.sharding import PartitionSpec as P

PLANES = 73
VHIDDEN = 256
MICRO = 4
EPSILON = 1e-05
F32, BF16 = jnp.float32, jnp.bfloat16
PRECISE = lax.Precision.HIGHEST
MESH = pl.DeviceIdType.MESH
LANES = 128
ILLEGAL = -1e30

FOLD, WIDE, PITCH = 4, 8, 10


def sigmoid(v):
    return 0.5 * jnp.tanh(0.5 * v) + 0.5


def silu_slope(v):
    s = sigmoid(v)
    return s * (1.0 + v * (1.0 - s))


def fold8(v):
    return jnp.sum(v.reshape(v.shape[0] // 8, 8, v.shape[1]), axis=0)


def total(v):
    return jnp.sum(v, axis=0, keepdims=True)


def kernel(
    n_dp, per, groups, moves, scale,
    policy, value_goal, board, weights, gains, head_conv, hidden_w, head_vec, legal,
    tap_grad, norm_grad, hc_grad, hw_grad, hv_grad, entry_grad,
    W, X, I, Z, C, B, raw, mask_raw, code, planes, turn, goal, vgoal, stage, stat, slots, back, mine, theirs,
    load_sem, send_sem, recv_sem, out_sem, swap_sem,
):
    core, me = lax.axis_index("pipe"), lax.axis_index("dp")
    block = 2 * per
    span = WIDE * block
    rows = FOLD * span
    channels = X.shape[-1]
    taps = 9 * channels
    all_rows = n_dp * rows

    barrier = pltpu.get_barrier_semaphore()

    def greet(j, carry):
        pl.semaphore_signal(barrier, inc=1, device_id=(core, lax.rem(me + j, n_dp)), device_id_type=MESH)
        return carry

    lax.fori_loop(1, n_dp, greet, 0)
    pl.semaphore_signal(barrier, inc=1, device_id=(1 - core, me), device_id_type=MESH)

    first = pl.multiple_of(core * groups * per, 8)
    loads = [
        pltpu.make_async_copy(board.at[pl.ds(first, groups * per)], raw, load_sem.at[0]),
        pltpu.make_async_copy(legal.at[pl.ds(first, groups * per)], mask_raw, load_sem.at[1]),
        pltpu.make_async_copy(weights, W, load_sem.at[2]),
    ]
    for load in loads:
        load.start()

    edge = jnp.zeros((block, channels), BF16)

    def clear(i, carry):
        for f in range(FOLD + 2):
            for column in (0, WIDE + 1):
                at = pl.ds((f * PITCH + column) * block, block)
                for g in range(groups):
                    X[i, g, at, :] = edge
                    I[i, g, at, :] = edge
                    Z[g, at, :] = edge
        return carry

    lax.fori_loop(0, 2, clear, 0)

    def put(ref, at, f, q, y):
        ref[*at, pl.ds(pl.multiple_of(((f + 1) * PITCH + 1 + q) * block, 16), block), :] = y.astype(BF16)
        none = jnp.zeros((per, channels), F32)
        if f == FOLD - 1:
            halo = jnp.concatenate([none, y[:per]], axis=0)
            ref[*at, pl.ds(pl.multiple_of((1 + q) * block, 16), block), :] = halo.astype(BF16)
        if f == 0:
            halo = jnp.concatenate([y[per:], none], axis=0)
            ref[*at, pl.ds(pl.multiple_of(((FOLD + 1) * PITCH + 1 + q) * block, 16), block), :] = halo.astype(BF16)

    def inside(f, q):
        return pl.ds(pl.multiple_of(((f + 1) * PITCH + 1 + q) * block, 16), block)

    def plain(f, q):
        return pl.ds(pl.multiple_of((f * WIDE + q) * block, 16), block)

    def each(body, carry=0):
        def column(q, carry):
            for f in range(FOLD):
                carry = body(f, q, carry)
            return carry

        return lax.fori_loop(0, WIDE, column, carry)

    loads[0].wait()
    for g in range(groups):

        def widen(b, carry, g=g):
            rows_of = raw[g * per + b].astype(F32).reshape(64, channels)
            for i in range(channels // LANES):
                turn[i, pl.ds(pl.multiple_of(b * 64, 64), 64), :] = rows_of[:, i * LANES : (i + 1) * LANES]
            return carry

        lax.fori_loop(0, per, widen, 0)

        def reorder(f, q, carry, g=g):
            parts = [
                jnp.concatenate(
                    [turn[i, pl.ds((f + FOLD * half) * 8 + q, per, stride=64), :] for half in range(2)], axis=0
                )
                for i in range(channels // LANES)
            ]
            put(X, (0, g), f, q, jnp.concatenate(parts, axis=1))
            return carry

        each(reorder)

    both = groups * per
    row_of = lax.broadcasted_iota(jnp.int32, (both, LANES), 0)
    lane_of = lax.broadcasted_iota(jnp.int32, (both, LANES), 1)

    def column_of(ref, zero):
        def pick(b, acc):
            return jnp.where(row_of == b, ref[first + b], acc)

        return lax.fori_loop(0, both, pick, zero)

    goal[...] = column_of(policy, jnp.zeros((both, LANES), jnp.int32))
    vgoal[...] = column_of(value_goal, jnp.zeros((both, LANES), F32))
    loads[1].wait()
    for square in range(64):
        base = square * PLANES // LANES * LANES
        shift = square * PLANES - base
        width = min(2 * LANES, moves - base)
        window = mask_raw[:, base : base + width]
        if width < 2 * LANES:
            window = jnp.concatenate([window, jnp.zeros((both, 2 * LANES - width), jnp.int32)], axis=1)
        if shift:
            window = pltpu.roll(window, 2 * LANES - shift, axis=1)
        window = window[:, :LANES]
        hit = goal[...] == lane_of + square * PLANES
        kind = jnp.where(hit, 2.0, jnp.where(window > 0, 1.0, 0.0))
        kind = jnp.where(lane_of < PLANES, kind, 0.0)
        f, q, half = square // 8 % FOLD, square % 8, square // 8 // FOLD
        at = ((f * WIDE + q) * 2 + half) * per
        for g in range(groups):
            code[g, pl.ds(at, per), :] = kind[g * per : (g + 1) * per]

    hc_grad[...] = jnp.zeros_like(hc_grad)
    hw_grad[...] = jnp.zeros_like(hw_grad)
    hv_grad[...] = jnp.zeros_like(hv_grad)
    norm_grad[...] = jnp.zeros_like(norm_grad)

    pl.semaphore_wait(barrier, n_dp)
    loads[2].wait()

    def push(k, g, top, bottom):
        slots[k, g, me, pl.ds(0, 1), :] = top
        slots[k, g, me, pl.ds(1, 1), :] = bottom

        def send(j, carry):
            pltpu.make_async_remote_copy(
                src_ref=slots.at[k, g, me],
                dst_ref=slots.at[k, g, me],
                send_sem=send_sem.at[k, g],
                recv_sem=recv_sem.at[k, g],
                device_id=(core, lax.rem(me + j, n_dp)),
                device_id_type=MESH,
            ).start()
            return carry

        lax.fori_loop(1, n_dp, send, 0)

    def arrived(k, g):
        others = slots.at[k, g, pl.ds(0, n_dp - 1)]
        copy = pltpu.make_async_remote_copy(
            src_ref=others, dst_ref=others, send_sem=send_sem.at[k, g], recv_sem=recv_sem.at[k, g],
            device_id=(core, lax.rem(me + 1, n_dp)), device_id_type=MESH,
        )
        copy.wait_send()
        copy.wait_recv()
        return slots[k, g]

    def merge_moments(k, g):
        parts = arrived(k, g)
        both_sums = jnp.sum(parts, axis=0)
        mean = both_sums[0:1] / n_dp
        apart = parts - mean
        between = jnp.sum(apart * apart, axis=0)[0:1]
        spread = (both_sums[1:2] + between * rows) / all_rows
        stat[k, g, pl.ds(0, 1), :] = mean
        stat[k, g, pl.ds(1, 1), :] = lax.rsqrt(spread + EPSILON)

    def norm_of(section, c, g):
        k = 2 * section + c
        gain = gains[section, pl.ds(c, 1), :]
        shift = gains[section, pl.ds(2 + c, 1), :]
        return stat[k, g, pl.ds(0, 1), :], stat[k, g, pl.ds(1, 1), :], gain, shift

    def convolve(field, section, c, g):
        k = 2 * section + c
        sums, parts = [], []
        for f in range(FOLD):
            slabs = [
                field[section, g, pl.ds(((f + t // 3) * PITCH + t % 3) * block, span), :] for t in range(9)
            ]
            out = jnp.dot(
                jnp.concatenate(slabs, axis=1), W[section, pl.ds(c * taps, taps), :],
                preferred_element_type=F32,
            )
            C[section, c, g, pl.ds(f * span, span), :] = out
            part = total(fold8(out))
            apart = out - part / span
            sums.append(part)
            parts.append(total(fold8(apart * apart)))
        mean = sum(sums) / rows
        spread = sum(parts)
        for part in sums:
            spread = spread + span * jnp.square(part / span - mean)
        push(k, g, mean, spread)

    def inner(section, g):
        mean, inv, gain, shift = norm_of(section, 0, g)
        factor = inv * gain

        def body(f, q, carry):
            v = (C[section, 0, g, plain(f, q), :] - mean) * factor + shift
            put(I, (section, g), f, q, v * sigmoid(v))
            return carry

        each(body)

    def outer_pre(section, g, f, q, norm):
        mean, inv, gain, shift = norm
        z = (C[section, 1, g, plain(f, q), :] - mean) * inv
        return X[section, g, inside(f, q), :].astype(F32) + z * gain + shift, z

    for g in range(groups):
        convolve(X, 0, 0, g)
    for section in range(2):
        for g in range(groups):
            merge_moments(2 * section, g)
            inner(section, g)
            convolve(I, section, 1, g)
        if section == 0:
            for g in range(groups):
                merge_moments(1, g)
                norm = norm_of(0, 1, g)

                def hand_on(f, q, carry, g=g, norm=norm):
                    v, _ = outer_pre(0, g, f, q, norm)
                    put(X, (1, g), f, q, v * sigmoid(v))
                    return carry

                each(hand_on)
                convolve(X, 1, 0, g)

    lane = lax.broadcasted_iota(jnp.int32, (per, LANES), 1)

    def heads(g):
        norm = norm_of(1, 1, g)

        def last(f, q, carry):
            v, _ = outer_pre(1, g, f, q, norm)
            B[g, plain(f, q), :] = v * sigmoid(v)
            return carry

        each(last)
        for f in range(FOLD):
            at = pl.ds(f * span, span)
            planes[at, :] = jnp.dot(B[g, at, :], head_conv[...], precision=PRECISE, preferred_element_type=F32)

        def look(f, q, carry):
            top, squares = carry
            a = planes[plain(f, q), :]
            a_legal = jnp.where(code[g, plain(f, q), :] > 0, a, ILLEGAL)
            top = jnp.maximum(top, jnp.maximum(a_legal[:per], a_legal[per:]))
            column = a[:, PLANES : PLANES + 1]
            for half in range(2):
                here = lane == (f + FOLD * half) * 8 + q
                squares = jnp.where(here, column[half * per : (half + 1) * per], squares)
            return top, squares

        top, pre = each(look, (jnp.full((per, LANES), ILLEGAL, F32), jnp.zeros((per, LANES), F32)))
        top = jnp.max(top, axis=1, keepdims=True)
        top = jnp.concatenate([top, top], axis=0)

        def weigh(f, q, acc):
            a = planes[plain(f, q), :]
            e = jnp.where(code[g, plain(f, q), :] > 0, jnp.exp(a - top), 0.0)
            planes[plain(f, q), :] = e
            return acc + e[:per] + e[per:]

        norm_sum = jnp.sum(each(weigh, jnp.zeros((per, LANES), F32)), axis=1, keepdims=True)
        portion = scale / norm_sum
        portion = jnp.concatenate([portion, portion], axis=0)

        squares = pre * sigmoid(pre)
        bias, out_w = head_vec[pl.ds(0, 1), :], head_vec[pl.ds(1, 1), :]
        hidden_pre = jnp.dot(squares, hidden_w[...], precision=PRECISE, preferred_element_type=F32) + bias
        hidden = hidden_pre * sigmoid(hidden_pre)
        value = jnp.tanh(jnp.sum(hidden * out_w, axis=1, keepdims=True))
        wanted = vgoal[pl.ds(g * per, per), 0:1]
        slope = 2.0 * scale * (value - wanted) * (1.0 - value * value)
        hidden_grad = slope * out_w * silu_slope(hidden_pre)
        hw_grad[...] += lax.dot_general(
            squares, hidden_grad, (((0,), (0,)), ((), ())), precision=PRECISE, preferred_element_type=F32
        )
        hv_grad[pl.ds(0, 1), :] += total(hidden_grad)
        hv_grad[pl.ds(1, 1), :] += total(hidden * slope)
        squares_grad = lax.dot_general(
            hidden_grad, hidden_w[...], (((1,), (1,)), ((), ())), precision=PRECISE, preferred_element_type=F32
        )
        pre_grad = squares_grad * silu_slope(pre)

        def slopes(f, q, carry):
            e = planes[plain(f, q), :] * portion
            e = e - jnp.where(code[g, plain(f, q), :] > 1.5, scale, 0.0)
            columns = [
                jnp.sum(jnp.where(lane == (f + FOLD * half) * 8 + q, pre_grad, 0.0), axis=1, keepdims=True)
                for half in range(2)
            ]
            column = jnp.concatenate(columns, axis=0)
            wide = lax.broadcasted_iota(jnp.int32, (block, LANES), 1)
            planes[plain(f, q), :] = jnp.where(wide == PLANES, column, e)
            return carry

        each(slopes)
        hc_grad[...] += lax.dot_general(
            B[g], planes[...], (((0,), (0,)), ((), ())), precision=PRECISE, preferred_element_type=F32
        )
        for f in range(FOLD):
            at = pl.ds(f * span, span)
            B[g, at, :] = lax.dot_general(
                planes[at, :], head_conv[...], (((1,), (1,)), ((), ())), precision=PRECISE,
                preferred_element_type=F32,
            )

    def outer_grad(section, g):
        norm = norm_of(section, 1, g)

        def body(f, q, carry):
            shift_sum, gain_sum = carry
            v, z = outer_pre(section, g, f, q, norm)
            grad = B[g, plain(f, q), :]
            if section == 0:
                grad = grad.astype(BF16).astype(F32)
            grad = grad * silu_slope(v)
            B[g, plain(f, q), :] = grad
            return shift_sum + fold8(grad), gain_sum + fold8(grad * z)

        zero = jnp.zeros((8, channels), F32)
        shift_sum, gain_sum = each(body, (zero, zero))
        push(4 + 2 * section + 1, g, total(shift_sum), total(gain_sum))

    def norm_back(section, c, g):
        sums = jnp.sum(arrived(4 + 2 * section + c, g), axis=0)
        norm_grad[pl.ds(4 * section + c, 1), :] += sums[1:2]
        norm_grad[pl.ds(4 * section + 2 + c, 1), :] += sums[0:1]
        mean, inv, gain, _ = norm_of(section, c, g)
        p_mean, pz_mean = sums[0:1] / all_rows, sums[1:2] / all_rows
        factor = inv * gain

        def body(f, q, carry):
            z = (C[section, c, g, plain(f, q), :] - mean) * inv
            p = B[g, plain(f, q), :] if c else C[section, 1, g, plain(f, q), :]
            put(Z, (g,), f, q, factor * (p - p_mean - z * pz_mean))
            return carry

        each(body)

    def back_field(section, c, g, f):
        acc = None
        for t in range(9):
            part = lax.dot_general(
                Z[g, pl.ds(((f + 2 - t // 3) * PITCH + 2 - t % 3) * block, span), :],
                W[section, pl.ds(c * taps + t * channels, channels), :],
                (((1,), (1,)), ((), ())), preferred_element_type=F32,
            )
            acc = part if acc is None else acc + part
        return acc

    def inner_grad(section, g):
        for f in range(FOLD):
            C[section, 1, g, pl.ds(f * span, span), :] = back_field(section, 1, g, f)
        mean, inv, gain, shift = norm_of(section, 0, g)

        def body(f, q, carry):
            shift_sum, gain_sum = carry
            z = (C[section, 0, g, plain(f, q), :] - mean) * inv
            grad = C[section, 1, g, plain(f, q), :] * silu_slope(z * gain + shift)
            C[section, 1, g, plain(f, q), :] = grad
            return shift_sum + fold8(grad), gain_sum + fold8(grad * z)

        zero = jnp.zeros((8, channels), F32)
        shift_sum, gain_sum = each(body, (zero, zero))
        push(4 + 2 * section, g, total(shift_sum), total(gain_sum))

    def entry(section, g):
        for f in range(FOLD):
            at = pl.ds(f * span, span)
            B[g, at, :] = B[g, at, :] + back_field(section, 0, g, f)

    def tap_gradient(section, c):
        field = I if c else X
        dz = jnp.concatenate(
            [Z[g, pl.ds(((f + 1) * PITCH + 1) * block, span), :] for g in range(groups) for f in range(FOLD)], axis=0
        )
        for t in range(9):
            moved = jnp.concatenate(
                [
                    field[section, g, pl.ds(((f + t // 3) * PITCH + t % 3) * block, span), :]
                    for g in range(groups)
                    for f in range(FOLD)
                ],
                axis=0,
            )
            grad = lax.dot_general(moved, dz, (((0,), (0,)), ((), ())), preferred_element_type=F32)
            stage[section, pl.ds(c * taps + t * channels, channels), :] = grad.astype(BF16)
        at = pl.ds(c * taps, taps)
        pltpu.make_async_copy(stage.at[section, at], tap_grad.at[section, at], out_sem.at[section, c]).start()

    for g in range(groups):
        merge_moments(3, g)
        heads(g)
        outer_grad(1, g)
    for section in (1, 0):
        for g in range(groups):
            norm_back(section, 1, g)
            inner_grad(section, g)
        tap_gradient(section, 1)
        for g in range(groups):
            norm_back(section, 0, g)
            if section == 1:
                entry(section, g)
                outer_grad(0, g)
        tap_gradient(section, 0)
    for g in range(groups):
        entry(0, g)

        def restore(f, q, carry, g=g):
            v = B[g, plain(f, q), :]
            for half in range(2):
                for i in range(channels // LANES):
                    part = v[half * per : (half + 1) * per, i * LANES : (i + 1) * LANES]
                    turn[i, pl.ds((f + FOLD * half) * 8 + q, per, stride=64), :] = part
            return carry

        each(restore)
        for f in range(FOLD):
            at = pl.ds(f * span, span)
            to = pl.ds(g * rows + f * span, span)
            mine[to, :] = turn[core, at, :].astype(BF16)
            theirs[to, :] = turn[1 - core, at, :].astype(BF16)
    own = pl.ds(pl.multiple_of(core * groups * rows, 16), groups * rows)
    swap = pltpu.make_async_remote_copy(
        src_ref=theirs, dst_ref=entry_grad.at[own], send_sem=swap_sem.at[0], recv_sem=swap_sem.at[1],
        device_id=(1 - core, me), device_id_type=MESH,
    )
    swap.start()
    keep = pltpu.make_async_copy(mine, entry_grad.at[own], swap_sem.at[2])
    keep.start()
    keep.wait()
    swap.wait()
    for section in range(2):
        for c in range(2):
            at = pl.ds(c * taps, taps)
            pltpu.make_async_copy(stage.at[section, at], tap_grad.at[section, at], out_sem.at[section, c]).wait()


def local(
    board_input, conv_weight, norm_gains, norm_shifts, head_params, policy_target, legal_mask, value_target
):
    n_dp, n_pipe = lax.axis_size("dp"), lax.axis_size("pipe")
    positions, channels = board_input.shape[0], board_input.shape[-1]
    per = positions // MICRO
    groups = MICRO // n_pipe
    moves = legal_mask.shape[1]
    rows = per * 64
    padded = (FOLD + 2) * PITCH * 2 * per
    taps = 9 * channels

    weights = lax.all_gather(lax.all_gather(conv_weight, "dp", axis=1, tiled=True), "pipe", axis=0, tiled=True)
    norms = jnp.stack([norm_gains, norm_shifts], axis=1)
    norms = lax.all_gather(lax.all_gather(norms, "dp", axis=2, tiled=True), "pipe", axis=0, tiled=True)
    norms = norms.astype(F32).reshape(2, 4, channels)
    norms = jnp.concatenate([norms, jnp.zeros_like(norms)], axis=1)
    head_all = lax.all_gather(head_params, ("pipe", "dp"), axis=0, tiled=True)
    conv_end = (PLANES + 1) * channels
    head_conv = jnp.pad(head_all[:conv_end].reshape(channels, PLANES + 1), ((0, 0), (0, LANES - PLANES - 1)))
    hidden_end = conv_end + 64 * VHIDDEN
    hidden_w = jnp.pad(head_all[conv_end:hidden_end].reshape(64, VHIDDEN), ((0, LANES - 64), (0, 0)))
    head_vec = jnp.pad(head_all[hidden_end:].reshape(2, VHIDDEN), ((0, 6), (0, 0)))

    vmem = pl.BlockSpec(memory_space=pltpu.VMEM)
    smem = pl.BlockSpec(memory_space=pltpu.SMEM)
    anywhere = pl.BlockSpec(memory_space=pl.ANY)
    dma, regular = pltpu.SemaphoreType.DMA, pltpu.VMEM
    tap_grad, norm_grad, hc_grad, hw_grad, hv_grad, entry_grad = pl.pallas_call(
        functools.partial(kernel, n_dp, per, groups, moves, 1.0 / positions),
        out_shape=(
            jax.ShapeDtypeStruct((2, 2 * taps, channels), BF16),
            jax.ShapeDtypeStruct((8, channels), F32),
            jax.ShapeDtypeStruct((channels, LANES), F32),
            jax.ShapeDtypeStruct((LANES, VHIDDEN), F32),
            jax.ShapeDtypeStruct((8, VHIDDEN), F32),
            jax.ShapeDtypeStruct((positions * 64, LANES), BF16),
        ),
        in_specs=[smem, smem, anywhere, anywhere, vmem, vmem, vmem, vmem, anywhere],
        out_specs=(anywhere, vmem, vmem, vmem, vmem, anywhere),
        scratch_shapes=[
            regular((2, 2 * taps, channels), BF16),
            regular((2, groups, padded, channels), BF16),
            regular((2, groups, padded, channels), BF16),
            regular((groups, padded, channels), BF16),
            regular((2, 2, groups, rows, channels), F32),
            regular((groups, rows, channels), F32),
            regular((groups * per, 8, 8, channels), BF16),
            regular((groups * per, moves), jnp.int32),
            regular((groups, rows, LANES), F32),
            regular((rows, LANES), F32),
            regular((channels // LANES, rows, LANES), F32),
            regular((groups * per, LANES), jnp.int32),
            regular((groups * per, LANES), F32),
            regular((2, 2 * taps, channels), BF16),
            regular((4, groups, 8, channels), F32),
            regular((8, groups, n_dp, 2, channels), F32),
            regular((8, LANES), F32),
            regular((groups * rows, LANES), BF16),
            regular((groups * rows, LANES), BF16),
            dma((3,)),
            dma((8, groups)),
            dma((8, groups)),
            dma((2, 2)),
            dma((3,)),
        ],
        compiler_params=pltpu.CompilerParams(
            collective_id=0, has_side_effects=True, vmem_limit_bytes=62 * 2**20
        ),
    )(policy_target, value_target, board_input, weights, norms, head_conv, hidden_w, head_vec, legal_mask)

    conv_grad = lax.psum_scatter(
        tap_grad.astype(F32).reshape(4 * taps, channels), ("pipe", "dp"), scatter_dimension=0, tiled=True
    )
    head_grad = jnp.concatenate(
        [hc_grad[:, : PLANES + 1].reshape(-1), hw_grad[:64].reshape(-1), hv_grad[:2].reshape(-1)]
    )
    head_grad = lax.psum_scatter(head_grad, ("pipe", "dp"), scatter_dimension=0, tiled=True)
    norm_grad = lax.psum(norm_grad, "pipe").reshape(2, 2, 2 * channels)[lax.axis_index("pipe")]
    width = norm_gains.shape[1]
    norm_grad = lax.dynamic_slice_in_dim(norm_grad, lax.axis_index("dp") * width, width, axis=1)
    entry_grad = entry_grad.astype(F32).reshape(positions, 8, 8, LANES)
    return conv_grad[None], norm_grad[:1], norm_grad[1:], head_grad, entry_grad


def solution(mesh):
    placed = (
        P("dp", None, None, None),
        P("pipe", "dp", None),
        P("pipe", "dp"),
        P("pipe", "dp"),
        P(("pipe", "dp")),
        P("dp"),
        P("dp", None),
        P("dp"),
    )
    return jax.shard_map(
        local,
        mesh=mesh,
        in_specs=placed,
        out_specs=(
            P("pipe", "dp", None),
            P("pipe", "dp"),
            P("pipe", "dp"),
            P(("pipe", "dp")),
            P("dp", None, None, "pipe"),
        ),
        check_vma=False,
    )
```

time: 1930 us -> 542 us (0.28)
  blocking collectives: 1180 us -> 44.4 us
  matrix products: 216 us -> 0 us
  waiting for transfers between devices: 184 us -> 340 us
  local copies, waits for them, and re-layouts: 157 us -> 12.4 us
  other arithmetic: 145 us -> 9.75 us
  Pallas kernels: 0 us -> 110 us
    psum x30 -> x1, blocking collectives: 1130 us -> 2.51 us  [local(): lax.psum(norm_grad, 'pipe').reshape(2, 2, 2 * channels)]
    dot_general x310 -> x0, matrix products: 216 us -> none  [the longest x90 58 us: convolve_back(): jnp.einsum('rd,cd->rc', grad_rows, tap_weights[offset], preferred_element...]
    pallas_call x0 -> x1, Pallas kernels: none -> 110 us  [local(): pl.pallas_call(functools.partial(kernel, n_dp, per, groups, moves, 1.0 /...]
    all_gather x1, waiting for transfers between devices: 0.01 us -> 66.3 us  [local(): lax.all_gather(conv_weight, 'dp', axis=1, tiled=True)]
    unnamed x6 -> x7, waiting for transfers between devices: 69.8 us -> 131 us
    unnamed x435 -> x13, local copies, waits for them, and re-layouts: 66.1 us -> 5.92 us
    reduce_sum x35 -> x0, other arithmetic: 49.5 us -> none  [the longest x10 16.5 us: statistics(): jnp.sum(jnp.square(field_map - average), axis=(0, 1, 2))]
    convert_element_type x21 -> x0, other arithmetic: 44 us -> none  [the longest x10 23.3 us: norm_backward(): return (result.astype(jnp.bfloat16), local_gain, local_shift)]
  transfers between devices with their start and end apart: 13 -> 5, of which waited for: 2 -> 4; matrix products, arithmetic and copies ran while one was open for 11% -> 3% of each run, Pallas kernels for 0% -> 0%
where the time goes in v1:
time: 542 us; the launch traced here: 533 us
  waiting for transfers between devices  340 us (63%)
  Pallas kernels  110 us (20%)
  blocking collectives  44.4 us (8%)
  between operations  16.2 us (3%)
  local copies, waits for them, and re-layouts  12.4 us (2%)
  other arithmetic  9.75 us (2%)
    reduce_scatter x1, waiting for transfers between devices, local(): lax.psum_scatter(tap_grad.astype(F32).reshape(4 * taps, channels), ('pipe...  143 us
    unnamed x7, waiting for transfers between devices  131 us
    pallas_call x1, Pallas kernels, local(): pl.pallas_call(functools.partial(kernel, n_dp, per, groups, moves, 1.0 /...  110 us
    all_gather x1, waiting for transfers between devices, local(): lax.all_gather(conv_weight, 'dp', axis=1, tiled=True)  66.3 us
    all_gather x1, blocking collectives, local(): lax.all_gather(norms, 'dp', axis=2, tiled=True)  40.1 us
  transfers between devices with their start and end apart: 5, of which 4 were waited for; matrix products, arithmetic and copies ran while one was open for 3% of the time, Pallas kernels for 0%

profile of v1, /device:TPU:0, one launch (start us, length us, event | category | flops | bytes accessed | tf_op | source)
XLA Modules:
  0.0 533.3 jit_solution(9255225992156463977)
XLA Ops:
  8.0 0.7 all-gather.3.cloned.1.call-update
  8.8 0.9 dynamic-update-slice
  9.7 0.7 copy-done.1
  10.5 66.3 %all-gather.3.cloned.1.call-done = bf16[1,4608,256]{2,1,0:T(8,128)(2,1)} async-done(((bf16[1,288,256]{2,1,0:T(8,128)(2,1)}), bf16[1,4608,256]{2,1,0:T(8,128)(2,1)}) %all-gather.3.cloned.1.call-update) | async-done | bytes 2359312 | tf_op jit(solution)/shard_map/all_gather | solution.py:499
  76.8 0.7 pad_maximum_fusion.1
  77.5 0.1 copy.13
  77.6 40.1 %all_gather.17 = bf16[1,2,512]{1,0,2:T(2,128)(2,1)S(1)} all-gather(bf16[1,2,32]{1,0,2:T(2,128)(2,1)S(1)} %copy.13), channel_id=1, replica_groups=mesh['pipe'=2,'dp'=16] {'dp'}, dimensions={2}, use_global_device_ids=true | all-gather | bytes 2176 | tf_op jit(solution)/shard_map/all_gather | solution.py:501
  117.7 0.1 copy.14
  117.8 1.8 all_gather.18
  119.6 0.6 pad_convert_fusion.gains
  120.2 23.5 %all-reduce.9.cloned.1.call-done = f32[35840]{0:T(1024)} async-done(((f32[35840]{0:T(1024)}), f32[35840]{0:T(1024)}) %all-reduce.9.cloned.1.call-update) | async-done | bytes 143376
  143.8 0.9 slice.62
  144.6 0.2 reshape.63
  144.8 0.7 pad.14.head_conv
  145.5 0.9 slice.63
  146.4 0.7 pad.15.hidden_w
  147.1 0.7 slice.64
  147.8 0.6 pad.16.head_vec
  148.4 110.5 %shard_map.119 = (bf16[2,4608,256]{2,1,0:T(8,128)(2,1)}, f32[8,256]{1,0:T(8,128)}, f32[256,128]{1,0:T(8,128)}, f32[128,256]{1,0:T(8,128)}, f32[8,256]{1,0:T(8,128)}, /*index=5*/bf16[6144,128]{1,0:T(8,128)(2,1)}) custom-call(s32[96]{0:T(128)} %policy.1, f32[96]{0:T(128)} %value_goal.1, bf16[96,8,8,256]{3,2,1,0:T(8,128)(2,1)} %board.1, ...), custom_call_target="tpu_custom_call" | custom-call | tf_op jit(solution)/shard_map/pallas_call | solution.py:515
  258.9 0.8 slice_bitcast_fusion
  259.8 1.0 reshape.67
  260.8 0.7 slice_bitcast_fusion.1
  261.5 0.7 pad_maximum_fusion
  262.3 5.7 %bitcast_convert_fusion = f32[9216,256]{1,0:T(8,128)} fusion(bf16[2,4608,256]{2,1,0:T(8,128)(2,1)} %get-tuple-element.11), kind=kLoop, calls=%fused_computation | loop fusion | flops 2359296 | bytes 14155776 | tf_op jit(solution)/shard_map/reshape | solution.py:559
  268.0 0.7 copy-done.2
  268.7 0.7 copy-done
  269.4 2.1 convert.6
  271.5 2.5 psum.7
  274.0 0.5 slice_bitcast_fusion.2
  274.6 106.7 %all-reduce.11.cloned.1.call-done = f32[35840]{0:T(1024)} async-done(((f32[35840]{0:T(1024)}), f32[35840]{0:T(1024)}) %all-reduce.11.cloned.1.call-update) | async-done | bytes 143376
  381.2 1.4 dynamic-slice.2
  382.6 142.7 %reduce-scatter.2.cloned.1.call-done = f32[288,256]{1,0:T(8,128)} async-done(((f32[9216,256]{1,0:T(8,128)}), f32[288,256]{1,0:T(8,128)}) %reduce-scatter.2.cloned.1.call-update) | async-done | bytes 294928 | tf_op jit(solution)/shard_map/reduce_scatter | solution.py:558
  (21 shorter events, 0.5 us)
Async XLA Ops:
  8.0 68.7 %all-gather.3.cloned.1.call-start = ((), (), s32[]{:S(2)}) async-start(), calls=%async_computation.1 | async-start | bytes 2506752 | tf_op jit(solution)/shard_map/all_gather | solution.py:499
  8.7 135.0 %all-reduce.9.cloned.1.call-start = ((), (), s32[]{:S(2)}) async-start(), calls=%async_computation.4 | async-start | bytes 286720
  9.7 0.7 copy-start.1
  10.4 138.0 %all-gather.5.cloned.1.call-start = ((), (), s32[]{:S(2)}) async-start(), calls=%async_computation.2 | async-start | bytes 7077888 | tf_op jit(solution)/shard_map/all_gather | solution.py:499
  76.8 304.5 %all-reduce.11.cloned.1.call-start = ((), (), s32[]{:S(2)}) async-start(), calls=%async_computation.5 | async-start | bytes 286720
  262.2 263.1 %reduce-scatter.2.cloned.1.call-start = ((), (), s32[]{:S(2)}) async-start(), calls=%async_computation.3 | async-start | bytes 9732096 | tf_op jit(solution)/shard_map/reduce_scatter | solution.py:558
  268.0 0.7 copy-start.2
  268.0 1.4 copy-start
Sparse Core Ops, SparseCore 0:
  11.6 65.0 all-gather.2
  78.3 13.3 all-gather.4
Sparse Core Ops, SparseCore 1:
  15.3 128.4 all-reduce.8
  262.3 118.9 all-reduce.10
  387.6 137.7 reduce-scatter.1
